TPU v7x, 1024 devices: a whole 8x8x8 slice. The times are simulated.
1024 devices in a mesh: sec: 256 (over y, z, x_hi, core), row: 4 (over x_lo).
Axes of the slice: x: 8 (x_hi: 2, x_lo: 4; x = x_hi * 4 + x_lo), y: 8, z: 8, core: 2. Of those that a mesh axis runs over, the one named last changes fastest.
Arguments:
- section_images: bfloat16 [256, 512, 512], P('sec', 'row'), may hold values from -6 to 6
- displacement: float32 [2, 256, 4, 4], P(None, 'sec', 'row'), may hold values from -2 to 2
- fold_mask: int32 [2, 256, 4, 4], P(None, 'sec', 'row'), may hold values 0 or 1
Outputs:
- relaxed_field: float32 [2, 256, 4, 4], P(None, 'sec', 'row')
- mean_offsets: float32 [2, 256, 4, 4], P(None, 'sec', 'row')
All inputs are finite; a program needn't handle non-finite values. No bound on the sum of `fold_mask` on one device may be relied on, other than what follows from the above.
Results may differ from a plain program's by a relative error of at most 0.0003.
Values may be sent and summed in bfloat16 or wider, within the bound.
A program may use at most 32 MiB of HBM per device.

v0:
```python
import functools
import math

import jax
import jax.numpy as jnp
import numpy as np
from jax import lax
from jax.experimental import pallas as pl
from jax.experimental.pallas import tpu as pltpu
from jax.sharding import PartitionSpec as P

SIZE = 128
HALF = 64
ITERS = 3
STEP = 0.5
STIFF = 0.2
EPS = 1e-6
SHARP = 0.5 * SIZE
F32 = jnp.float32
BF16 = jnp.bfloat16
COORD = pl.DeviceIdType.MESH

NEAR = [(1, 0), (-1, 0)]
PEERS = NEAR + [(0, 1), (0, -1), (1, 1), (1, -1), (-1, 1), (-1, -1), (2, 0), (-2, 0)]
SLOT = {peer: k for k, peer in enumerate(PEERS)}


def split_table(table):
    high = table.astype(jnp.bfloat16)
    low = (table - high.astype(np.float64)).astype(jnp.bfloat16)
    return high, low


def make_tables():
    index = np.arange(SIZE)
    angles = (index[:, None] * index[None, :] % SIZE) * (2.0 * math.pi / SIZE)
    cosines, sines = np.cos(angles), np.sin(angles)
    sign = np.where(index % 2 == 0, 1.0, -1.0)
    real = cosines[:, :HALF]
    imag = -sines[:, :HALF].copy()
    imag[:, 0] = sign
    zero = np.zeros((SIZE, HALF))
    along_x = np.block([[real, zero, imag, zero], [zero, real, zero, imag]])
    along_u = np.block([[cosines, -sines], [sines, cosines]])
    back_real = 2.0 * cosines[:HALF]
    back_real[0] = 1.0
    back_imag = -2.0 * sines[:HALF]
    back_imag[0] = sign
    wide = np.zeros((HALF, SIZE))
    along_v = np.block(
        [[back_real, wide], [wide, back_real], [back_imag, wide], [wide, back_imag]]
    )
    parts = []
    for table in (along_x, along_u, along_v):
        parts.extend(split_table(table))
    return np.stack(parts)


def fit_even(function, terms):
    nodes = 0.25 * (0.5 + 0.5 * np.cos(np.pi * (np.arange(200) + 0.5) / 200))
    powers = np.vander(nodes * 4.0, terms, increasing=True)
    solved = np.linalg.lstsq(powers, function(np.sqrt(nodes)), rcond=None)[0]
    return [float(c) for c in solved * 4.0 ** np.arange(terms)]


SIN_FIT = fit_even(lambda r: np.sin(np.pi * r) / r, 6)
COS_FIT = fit_even(lambda r: np.cos(np.pi * r), 7)


def horner(coefficients, value):
    total = coefficients[-1]
    for c in coefficients[-2::-1]:
        total = total * value + c
    return total


def turn(turns):
    r = turns - jnp.round(turns)
    squared = r * r
    s = r * horner(SIN_FIT, squared)
    c = horner(COS_FIT, squared)
    return 1.0 - 2.0 * s * s, 2.0 * s * c


def halves(values):
    high = values.astype(BF16)
    return high, (values - high.astype(F32)).astype(BF16)


def dot(a, b):
    return jnp.dot(a, b, preferred_element_type=F32)


def left_product(table, values):
    high, low = halves(values)
    return dot(table[0], high) + (dot(table[0], low) + dot(table[1], high))


def right_product(values, table):
    high, low = halves(values)
    return dot(high, table[0]) + (dot(low, table[0]) + dot(high, table[1]))


def iota(shape, dim):
    return lax.broadcasted_iota(jnp.int32, shape, dim)


def spectrum(image, along_x, along_u):
    rows = jnp.concatenate([image[:, :256], image[:, 256:]], axis=0)
    first = dot(rows, along_x[0]) + dot(rows, along_x[1])
    real = jnp.concatenate([first[:SIZE, :SIZE], first[SIZE:, :SIZE]], axis=1)
    imag = jnp.concatenate([first[:SIZE, SIZE:], first[SIZE:, SIZE:]], axis=1)
    edge = iota((SIZE, 256), 1) % HALF == 0
    main = jnp.concatenate([real, jnp.where(edge, 0.0, -imag)], axis=0)
    last = jnp.where(edge, imag, 0.0)
    full = left_product(along_u, main)
    nyquist = left_product((along_u[0][:, :SIZE], along_u[1][:, :SIZE]), last)
    constant = edge & (iota((SIZE, 256), 0) == 0)
    full_real = jnp.where(constant, 0.0, full[:SIZE])
    full_imag = jnp.where(constant, 0.0, full[SIZE:])
    return full_real, full_imag, nyquist[:SIZE], nyquist[SIZE:]


def column_sums(values):
    middle = values[HALF : HALF + 1]
    return jnp.sum(values, axis=0, keepdims=True) - middle, middle


def energy_rows(spec):
    real, imag, edge_real, edge_imag = spec
    weight = jnp.where(iota((SIZE, 256), 1) % HALF == 0, 1.0, 2.0)
    rows = iota((SIZE, 256), 0)
    out = []
    for power in (weight * (real * real + imag * imag), edge_real * edge_real + edge_imag * edge_imag):
        out.append(jnp.sum(jnp.where(rows == HALF, 0.0, power), axis=0, keepdims=True))
        out.append(power[HALF : HALF + 1])
    return out


def to_lanes(rows):
    lane = iota((rows.shape[0], SIZE), 1)
    left, right = rows[:, :SIZE], rows[:, SIZE:]
    total = jnp.zeros((rows.shape[0], SIZE), F32)
    for c, (part, low) in enumerate([(left, True), (left, False), (right, True), (right, False)]):
        kept = jnp.where((lane < HALF) == low, part, 0.0)
        total = total + jnp.where(lane == c, jnp.sum(kept, axis=1, keepdims=True), 0.0)
    return total


def from_lanes(rows):
    shape = (rows.shape[0], SIZE)
    lane = iota(shape, 1)
    spread = [jnp.broadcast_to(rows[:, c : c + 1], shape) for c in range(4)]
    return jnp.concatenate(
        [
            jnp.where(lane < HALF, spread[0], spread[1]),
            jnp.where(lane < HALF, spread[2], spread[3]),
        ],
        axis=1,
    )


def stack(rows):
    width = rows[0].shape[1]
    pad = -len(rows) % 8
    return jnp.concatenate(rows + [jnp.zeros((1, width), F32)] * pad, axis=0)


def prepare(own, other):
    ar, ai, aer, aei = own
    br, bi, ber, bei = other
    cross_real = ar * br + ai * bi
    cross_imag = ar * bi - ai * br
    edge_real = aer * ber + aei * bei
    edge_imag = aer * bei - aei * ber
    rows = energy_rows(own) + energy_rows(other)
    rows = [row * (1.0 / (SIZE * SIZE)) for row in rows] + [edge_real[HALF : HALF + 1]]
    return cross_real - edge_imag, cross_imag + edge_real, to_lanes(stack(rows))


def sums_of_lags(field_own, field_other, cross_real, cross_imag, terms, along_u, along_v):
    dy_own, dy_other = field_own, field_other
    dx_own = pltpu.roll(field_own, SIZE - 4, 1)
    dx_other = pltpu.roll(field_other, SIZE - 4, 1)
    cosines, _ = turn(
        0.5 * stack([dy_own, dx_own, dy_own + dx_own, dy_other, dx_other, dy_other + dx_other])
    )
    squares = cosines * cosines
    energy_own = terms[0:1] + squares[0:1] * terms[1:2] + squares[1:2] * terms[2:3] + squares[2:3] * terms[3:4]
    energy_other = terms[4:5] + squares[3:4] * terms[5:6] + squares[4:5] * terms[6:7] + squares[5:6] * terms[7:8]
    scale = (SHARP / (SIZE * SIZE)) / jnp.sqrt(energy_own * energy_other + EPS)
    factor_y = cosines[0:1] * cosines[3:4]
    factor_x = cosines[1:2] * cosines[4:5]
    corner = (cosines[2:3] * cosines[5:6] - factor_y * factor_x) * terms[8:9]
    spread = from_lanes(
        stack(
            [
                (dy_own - dy_other) * (-1.0 / SIZE),
                (dx_own - dx_other) * (-1.0 / SIZE),
                factor_y,
                factor_x * scale,
                scale,
                corner * scale,
            ]
        )
    )
    u = iota((SIZE, 256), 0)
    signed_u = jnp.where(u >= HALF, u - SIZE, u).astype(F32)
    turn_cos, turn_sin = turn(signed_u * spread[0:1])
    turn_cos = jnp.where(u == HALF, spread[2:3], turn_cos)
    turn_sin = jnp.where(u == HALF, 0.0, turn_sin)
    shifted = jnp.concatenate(
        [
            cross_real * turn_cos - cross_imag * turn_sin,
            cross_real * turn_sin + cross_imag * turn_cos,
        ],
        axis=0,
    )
    columns = left_product(along_u, shifted)
    real, imag = columns[:SIZE], columns[SIZE:]
    v = iota((1, 256), 1) % HALF
    row_cos, row_sin = turn(v.astype(F32) * spread[1:2])
    row_cos = row_cos * spread[4:5]
    row_sin = row_sin * spread[4:5]
    row_cos_edge = jnp.where(v == 0, spread[3:4], row_cos)
    sign = (1 - 2 * (u % 2)).astype(F32)
    moved_real = real * row_cos - imag * row_sin
    moved_imag = real * row_sin + imag * row_cos_edge + sign * jnp.where(v == 0, spread[5:6], 0.0)
    pairs = jnp.concatenate(
        [
            jnp.concatenate([moved_real[:, :SIZE], moved_imag[:, :SIZE]], axis=1),
            jnp.concatenate([moved_real[:, SIZE:], moved_imag[:, SIZE:]], axis=1),
        ],
        axis=0,
    )
    weights = jnp.exp(right_product(pairs, along_v))

    b = iota((1, 256), 1) % SIZE
    signed_b = jnp.where(b >= HALF, b - SIZE, b).astype(F32)
    totals, moments_a, moments_b, ends_a, ends_b = [], [], [], [], []
    for g in range(2):
        block = weights[g * SIZE : (g + 1) * SIZE]
        total = jnp.sum(block, axis=0, keepdims=True)
        totals.append(total)
        moments_a.append(jnp.sum(block * signed_u, axis=0, keepdims=True))
        moments_b.append(total * signed_b)
        ends_a.append(block[HALF : HALF + 1])
        ends_b.append(jnp.where(b == HALF, total, 0.0))
    rows = stack(totals + moments_a + moments_b + ends_a + ends_b)
    k = iota((16, SIZE), 0)
    lane = iota((16, SIZE), 1)
    kind, g = k // 2, k % 2
    out = [0.0, 0.0, 0.0]
    for which in range(2):
        reduced = jnp.sum(rows[:, which * SIZE : (which + 1) * SIZE], axis=1, keepdims=True)
        here = (lane % 4 == 2 * g + which) & (lane < 8)
        component = lane // 4
        for n, chosen in enumerate(
            (kind == 0, kind == 1 + component, kind == 3 + component)
        ):
            out[n] = out[n] + jnp.sum(jnp.where(here & chosen, reduced, 0.0), axis=0, keepdims=True)
    return out


def kernel(
    images, displacement, fold_mask, tables, relaxed_ref, mean_ref,
    own_image, other_image, table, disp, mask, first, first_in, sent, received,
    load_sem, image_send, image_recv, first_send, first_recv, send_sem, recv_sem,
):
    section, row = lax.axis_index("sec"), lax.axis_index("row")
    sections, nrows = lax.axis_size("sec"), lax.axis_size("row")

    def device(peer):
        return (lax.rem(section + peer[0] + sections, sections), row + peer[1])

    def when_there(peer, action):
        if peer[1] == 0:
            action()
        else:
            pl.when((row + peer[1] >= 0) & (row + peer[1] < nrows))(action)

    barrier = pltpu.get_barrier_semaphore()
    for peer in PEERS:
        when_there(
            peer,
            lambda peer=peer: pl.semaphore_signal(
                barrier, inc=1, device_id=device(peer), device_id_type=COORD
            ),
        )
    loads = [
        pltpu.make_async_copy(displacement, disp, load_sem.at[0]),
        pltpu.make_async_copy(fold_mask, mask, load_sem.at[1]),
        pltpu.make_async_copy(images, own_image, load_sem.at[2]),
        pltpu.make_async_copy(tables, table, load_sem.at[3]),
    ]
    for load in loads:
        load.start()
    loads[0].wait()
    loads[1].wait()
    first[...] = jnp.zeros((1, SIZE), F32)
    for k in range(2):
        first[:, 4 * k : 4 * k + 4] = disp[k, 0]
        first[:, 8 + 4 * k : 12 + 4 * k] = mask[k, 0].astype(F32)

    inside = (row > 0).astype(jnp.int32) + (row < nrows - 1).astype(jnp.int32)
    pl.semaphore_wait(barrier, 4 + 3 * inside)

    image_copies, first_copies = [], []
    for k, peer in enumerate(NEAR):
        part = pl.ds(256 * (1 - k), 256)
        image_copies.append(
            pltpu.make_async_remote_copy(
                src_ref=images.at[:, part],
                dst_ref=other_image.at[:, part],
                send_sem=image_send.at[k],
                recv_sem=image_recv.at[1 - k],
                device_id=device(peer),
                device_id_type=COORD,
            )
        )
        first_copies.append(
            pltpu.make_async_remote_copy(
                src_ref=first,
                dst_ref=first_in.at[k],
                send_sem=first_send.at[k],
                recv_sem=first_recv.at[k],
                device_id=device(peer),
                device_id_type=COORD,
            )
        )
    for copy in image_copies + first_copies:
        copy.start()

    loads[2].wait()
    loads[3].wait()
    along_x, along_u, along_v = (
        (table[0], table[1]), (table[2], table[3]), (table[4], table[5])
    )
    own_spectrum = spectrum(own_image[...], along_x, along_u)

    for copy in first_copies:
        copy.wait_recv()
    lane = iota((1, SIZE), 1)
    column = lane % 4
    low = column < 2
    below, above, mine = first_in[0], first_in[1], first[...]

    def weights(values, position):
        aligned = pltpu.roll(values, SIZE - 8, 1)
        both = aligned * jnp.where(
            lane < 4, (position > 0).astype(F32), (position < sections - 1).astype(F32)
        )
        both = jnp.where(lane < 8, both, 0.0)
        lower = jnp.where(lane < 4, both, pltpu.roll(both, 4, 1))
        upper = jnp.where(lane < 4, pltpu.roll(both, SIZE - 4, 1), both)
        norm = 1.0 / jnp.maximum(lower + upper, 1.0)
        return jnp.where(lane < 8, lower * norm, 0.0), jnp.where(lane < 8, upper * norm, 0.0)

    lower_mine, upper_mine = weights(mine, section)
    lower_above, _ = weights(above, lax.rem(section + 1, sections))
    _, upper_below = weights(below, lax.rem(section + sections - 1, sections))
    coef_own = jnp.where(low, upper_mine, lower_mine)
    coef_other = jnp.where(low, lower_above, upper_below)
    field = jnp.where(lane < 8, mine, 0.0)
    field_other = jnp.where(lane < 8, jnp.where(low, above, below), 0.0)

    for copy in image_copies:
        copy.wait_recv()
    other_spectrum = spectrum(other_image[...], along_x, along_u)
    cross_real, cross_imag, terms = prepare(own_spectrum, other_spectrum)

    def left_of(values):
        return pltpu.roll(values, 1, 1)

    def right_of(values):
        return pltpu.roll(values, SIZE - 1, 1)

    copies = []
    for step in range(ITERS):
        last = step == ITERS - 1
        total, moment, end = sums_of_lags(
            field, field_other, cross_real, cross_imag, terms, along_u, along_v
        )
        total = jnp.where(lane < 8, total, 1.0)
        offset = moment / total
        mirrored = -offset - SIZE * (end / total)
        mean_own = coef_own * offset
        share = STEP * coef_other * mirrored
        sent[step, 0] = field + STEP * mean_own
        sent[step, 1] = share
        peers = [peer for peer in PEERS if abs(peer[0]) < 2] if last else PEERS

        def exchange(peer):
            return pltpu.make_async_remote_copy(
                src_ref=sent.at[step],
                dst_ref=received.at[step, SLOT[peer]],
                send_sem=send_sem.at[step, SLOT[peer]],
                recv_sem=recv_sem.at[step, SLOT[peer]],
                device_id=device(peer),
                device_id_type=COORD,
            )

        for peer in peers:
            when_there(peer, lambda peer=peer: exchange(peer).start())
        for peer in peers:
            opposite = (-peer[0], -peer[1])
            when_there(opposite, lambda peer=peer: exchange(peer).wait_recv())

        def base(ds, dr):
            if (ds, dr) == (0, 0):
                return sent[step, 0]
            return received[step, SLOT[(-ds, -dr)], 0]

        def shared(ds, dr):
            if (ds, dr) == (0, 0):
                return sent[step, 1]
            return received[step, SLOT[(-ds, -dr)], 1]

        there = {-1: row > 0, 1: row < nrows - 1}
        own_rows = {
            dr: base(0, dr) + jnp.where(low, shared(-1, dr), shared(1, dr)) for dr in (-1, 0, 1)
        }
        mine = own_rows[0]
        around = (
            jnp.where(there[-1], own_rows[-1], 0.0)
            + jnp.where(there[1], own_rows[1], 0.0)
            + jnp.where(column == 0, 0.0, left_of(mine))
            + jnp.where(column == 3, 0.0, right_of(mine))
        )
        smoothed = mine + STIFF * (around - 4.0 * mine)
        if last:
            mean = mean_own + (1.0 / STEP) * jnp.where(low, shared(-1, 0), shared(1, 0))
            for k in range(2):
                relaxed_ref[k, 0] = smoothed[:, 4 * k : 4 * k + 4]
                mean_ref[k, 0] = mean[:, 4 * k : 4 * k + 4]
        else:
            other_rows = {
                dr: jnp.where(low, base(1, dr), base(-1, dr)) + shared(0, dr) for dr in (-1, 0, 1)
            }
            across = jnp.where(
                column == 1, base(-1, 0) + shared(-2, 0), base(1, 0) + shared(2, 0)
            )
            them = other_rows[0]
            around = (
                jnp.where(there[-1], other_rows[-1], 0.0)
                + jnp.where(there[1], other_rows[1], 0.0)
                + jnp.where(
                    column == 0, 0.0, jnp.where(column == 2, left_of(across), left_of(them))
                )
                + jnp.where(
                    column == 3, 0.0, jnp.where(column == 1, right_of(across), right_of(them))
                )
            )
            field = jnp.where(lane < 8, smoothed, 0.0)
            field_other = jnp.where(lane < 8, them + STIFF * (around - 4.0 * them), 0.0)

    for copy in image_copies + first_copies:
        copy.wait_send()
    for step in range(ITERS):
        for peer in PEERS:
            if step == ITERS - 1 and abs(peer[0]) == 2:
                continue
            when_there(
                peer,
                lambda peer=peer, step=step: pltpu.make_async_remote_copy(
                    src_ref=sent.at[step],
                    dst_ref=received.at[step, SLOT[peer]],
                    send_sem=send_sem.at[step, SLOT[peer]],
                    recv_sem=recv_sem.at[step, SLOT[peer]],
                    device_id=device(peer),
                    device_id_type=COORD,
                ).wait_send(),
            )


def per_device(section_images, displacement, fold_mask):
    tables = jnp.asarray(make_tables())
    result = jax.ShapeDtypeStruct((2, 1, 1, 4), F32)
    return pl.pallas_call(
        kernel,
        out_shape=(result, result),
        in_specs=[pl.BlockSpec(memory_space=pl.ANY)] * 4,
        out_specs=[pl.BlockSpec(memory_space=pltpu.VMEM)] * 2,
        scratch_shapes=[
            pltpu.VMEM((SIZE, 512), BF16),
            pltpu.VMEM((SIZE, 512), BF16),
            pltpu.VMEM((6, 256, 256), BF16),
            pltpu.VMEM((2, 1, 1, 4), F32),
            pltpu.VMEM((2, 1, 1, 4), jnp.int32),
            pltpu.VMEM((1, SIZE), F32),
            pltpu.VMEM((2, 1, SIZE), F32),
            pltpu.VMEM((ITERS, 2, 1, SIZE), F32),
            pltpu.VMEM((ITERS, len(PEERS), 2, 1, SIZE), F32),
            pltpu.SemaphoreType.DMA((4,)),
            pltpu.SemaphoreType.DMA((2,)),
            pltpu.SemaphoreType.DMA((2,)),
            pltpu.SemaphoreType.DMA((2,)),
            pltpu.SemaphoreType.DMA((2,)),
            pltpu.SemaphoreType.DMA((ITERS, len(PEERS))),
            pltpu.SemaphoreType.DMA((ITERS, len(PEERS))),
        ],
        compiler_params=pltpu.CompilerParams(
            collective_id=0, has_side_effects=True, vmem_limit_bytes=32 * 1024 * 1024
        ),
    )(section_images[0], displacement, fold_mask, tables)


def solution(mesh):
    in_specs = (P("sec", "row", None), P(None, "sec", "row", None), P(None, "sec", "row", None))
    out_specs = (P(None, "sec", "row", None), P(None, "sec", "row", None))
    return jax.shard_map(
        per_device, mesh=mesh, in_specs=in_specs, out_specs=out_specs, check_vma=False
    )
```

profile of v0, /device:TPU:2, one launch (start us, length us, event | category | flops | bytes accessed | tf_op | source)
XLA Modules:
  0.0 60.8 jit_solution(17778860962841503979)
XLA Ops:
  0.6 0.0 copy-start.2
  0.6 0.7 %copy-done.2 = f32[2,1,1,4]{3,2,1,0:T(1,128)S(1)} copy-done((f32[2,1,1,4]{3,2,1,0:T(1,128)S(1)}, f32[2,1,1,4]{3,2,1,0:T(1,128)}, u32[]{:S(2)}) %copy-start.2) | copy-done | bytes 56
  1.3 0.0 copy-start
  1.3 1.1 %copy-done = bf16[6,256,256]{2,1,0:T(8,128)(2,1)S(1)} copy-done((bf16[6,256,256]{2,1,0:T(8,128)(2,1)S(1)}, bf16[6,256,256]{2,1,0:T(8,128)(2,1)}, u32[]{:S(2)}) %copy-start) | copy-done | bytes 786456
  2.4 0.0 copy-start.1
  2.4 0.9 %copy-done.1 = bf16[1,128,512]{2,1,0:T(8,128)(2,1)S(1)} copy-done((bf16[1,128,512]{2,1,0:T(8,128)(2,1)S(1)}, bf16[1,128,512]{2,1,0:T(8,128)(2,1)}, u32[]{:S(2)}) %copy-start.1) | copy-done | bytes 131096
  3.3 0.0 copy-start.3
  3.4 0.7 %copy-done.3 = s32[2,1,1,4]{3,2,1,0:T(1,128)S(1)} copy-done((s32[2,1,1,4]{3,2,1,0:T(1,128)S(1)}, s32[2,1,1,4]{3,2,1,0:T(1,128)}, u32[]{:S(2)}) %copy-start.3) | copy-done | bytes 56
  4.0 55.7 %shard_map.59 = (f32[2,1,1,4]{3,2,1,0:T(1,128)S(1)}, f32[2,1,1,4]{3,2,1,0:T(1,128)S(1)}) custom-call(bf16[128,512]{1,0:T(8,128)(2,1)S(1)} %bitcast.1, f32[2,1,1,4]{3,2,1,0:T(1,128)S(1)} %copy-done.2, s32[2,1,1,4]{3,2,1,0:T(1,128)S(1)} %copy-done.3, bf16[6,256,256]{2,1,0:T(8,128)(2,1)S(1)} %copy-done), custom_call_target="tpu_custom_call" | custom-call | tf_op jit(solution)/shard_map/pallas_call | solution.py:479
  59.7 0.6 copy.8
  60.3 0.6 copy.9
Async XLA Ops:
  0.6 0.7 %copy-start.2 = (f32[2,1,1,4]{3,2,1,0:T(1,128)S(1)}, f32[2,1,1,4]{3,2,1,0:T(1,128)}, u32[]{:S(2)}) copy-start(f32[2,1,1,4]{3,2,1,0:T(1,128)} %displacement.1) | copy-start | bytes 100
  1.3 1.1 %copy-start = (bf16[6,256,256]{2,1,0:T(8,128)(2,1)S(1)}, bf16[6,256,256]{2,1,0:T(8,128)(2,1)}, u32[]{:S(2)}) copy-start(bf16[6,256,256]{2,1,0:T(8,128)(2,1)} %constant.2.clone.tables) | copy-start | bytes 2359300
  2.4 0.9 %copy-start.1 = (bf16[1,128,512]{2,1,0:T(8,128)(2,1)S(1)}, bf16[1,128,512]{2,1,0:T(8,128)(2,1)}, u32[]{:S(2)}) copy-start(bf16[1,128,512]{2,1,0:T(8,128)(2,1)} %param.4) | copy-start | bytes 393220
  3.3 0.7 %copy-start.3 = (s32[2,1,1,4]{3,2,1,0:T(1,128)S(1)}, s32[2,1,1,4]{3,2,1,0:T(1,128)}, u32[]{:S(2)}) copy-start(s32[2,1,1,4]{3,2,1,0:T(1,128)} %fold_mask.1) | copy-start | bytes 100
where the time goes:
time: 61.1 us; the launch traced here: 60.8 us
  Pallas kernels  55.7 us (91%)
  local copies, waits for them, and re-layouts  4.51 us (7%)
  between operations  0.65 us (1%)
    pallas_call x1, Pallas kernels, per_device(): pl.pallas_call(kernel, out_shape=(result, result), in_specs=[pl.BlockSpec...  55.7 us
    unnamed x10, local copies, waits for them, and re-layouts  4.51 us

commit v1 on v0

--- a/solution.py
+++ b/solution.py
@@ -20,8 +20,8 @@
 BF16 = jnp.bfloat16
 COORD = pl.DeviceIdType.MESH
 
-NEAR = [(1, 0), (-1, 0)]
-PEERS = NEAR + [(0, 1), (0, -1), (1, 1), (1, -1), (-1, 1), (-1, -1), (2, 0), (-2, 0)]
+PEERS = [(1, 0), (-1, 0), (0, 1), (0, -1), (1, 1), (1, -1), (-1, 1), (-1, -1)]
+LAST_PEERS = [(-1, 0), (0, 1), (0, -1), (-1, 1), (-1, -1)]
 SLOT = {peer: k for k, peer in enumerate(PEERS)}
 
 
@@ -263,21 +263,25 @@
 
 
 def kernel(
-    images, displacement, fold_mask, tables, relaxed_ref, mean_ref,
+    images, displacement, fold_mask, tables, result_ref,
     own_image, other_image, table, disp, mask, first, first_in, sent, received,
-    load_sem, image_send, image_recv, first_send, first_recv, send_sem, recv_sem,
+    load_sem, image_sem, first_sem, send_sem, recv_sem,
 ):
     section, row = lax.axis_index("sec"), lax.axis_index("row")
     sections, nrows = lax.axis_size("sec"), lax.axis_size("row")
+    above, below = section < sections - 1, section > 0
+    there = {-1: row > 0, 1: row < nrows - 1}
 
     def device(peer):
-        return (lax.rem(section + peer[0] + sections, sections), row + peer[1])
+        return (section + peer[0], row + peer[1])
 
     def when_there(peer, action):
-        if peer[1] == 0:
-            action()
-        else:
-            pl.when((row + peer[1] >= 0) & (row + peer[1] < nrows))(action)
+        conditions = []
+        if peer[0] != 0:
+            conditions.append(above if peer[0] > 0 else below)
+        if peer[1] != 0:
+            conditions.append(there[peer[1]])
+        pl.when(functools.reduce(jnp.logical_and, conditions))(action)
 
     barrier = pltpu.get_barrier_semaphore()
     for peer in PEERS:
@@ -302,34 +306,34 @@
         first[:, 4 * k : 4 * k + 4] = disp[k, 0]
         first[:, 8 + 4 * k : 12 + 4 * k] = mask[k, 0].astype(F32)
 
-    inside = (row > 0).astype(jnp.int32) + (row < nrows - 1).astype(jnp.int32)
-    pl.semaphore_wait(barrier, 4 + 3 * inside)
-
-    image_copies, first_copies = [], []
-    for k, peer in enumerate(NEAR):
-        part = pl.ds(256 * (1 - k), 256)
-        image_copies.append(
-            pltpu.make_async_remote_copy(
-                src_ref=images.at[:, part],
-                dst_ref=other_image.at[:, part],
-                send_sem=image_send.at[k],
-                recv_sem=image_recv.at[1 - k],
-                device_id=device(peer),
-                device_id_type=COORD,
-            )
-        )
-        first_copies.append(
-            pltpu.make_async_remote_copy(
-                src_ref=first,
-                dst_ref=first_in.at[k],
-                send_sem=first_send.at[k],
-                recv_sem=first_recv.at[k],
-                device_id=device(peer),
-                device_id_type=COORD,
-            )
-        )
-    for copy in image_copies + first_copies:
-        copy.start()
+    def count(flag):
+        return flag.astype(jnp.int32)
+
+    along = count(above) + count(below)
+    beside = count(there[-1]) + count(there[1])
+    pl.semaphore_wait(barrier, along + beside + along * beside)
+
+    first_copy = pltpu.make_async_remote_copy(
+        src_ref=first,
+        dst_ref=first_in,
+        send_sem=first_sem.at[0],
+        recv_sem=first_sem.at[1],
+        device_id=device((1, 0)),
+        device_id_type=COORD,
+    )
+    image_copy = pltpu.make_async_remote_copy(
+        src_ref=images,
+        dst_ref=other_image,
+        send_sem=image_sem.at[0],
+        recv_sem=image_sem.at[1],
+        device_id=device((1, 0)),
+        device_id_type=COORD,
+    )
+
+    @pl.when(above)
+    def _():
+        first_copy.start()
+        image_copy.start()
 
     loads[2].wait()
     loads[3].wait()
@@ -338,12 +342,19 @@
     )
     own_spectrum = spectrum(own_image[...], along_x, along_u)
 
-    for copy in first_copies:
-        copy.wait_recv()
     lane = iota((1, SIZE), 1)
     column = lane % 4
-    low = column < 2
-    below, above, mine = first_in[0], first_in[1], first[...]
+
+    @pl.when(below)
+    def _():
+        first_copy.wait_recv()
+
+    @pl.when(jnp.logical_not(below))
+    def _():
+        first_in[...] = jnp.zeros((1, SIZE), F32)
+        other_image[...] = jnp.zeros((SIZE, 512), BF16)
+
+    mine, under = first[...], first_in[...]
 
     def weights(values, position):
         aligned = pltpu.roll(values, SIZE - 8, 1)
@@ -356,26 +367,38 @@
         norm = 1.0 / jnp.maximum(lower + upper, 1.0)
         return jnp.where(lane < 8, lower * norm, 0.0), jnp.where(lane < 8, upper * norm, 0.0)
 
-    lower_mine, upper_mine = weights(mine, section)
-    lower_above, _ = weights(above, lax.rem(section + 1, sections))
-    _, upper_below = weights(below, lax.rem(section + sections - 1, sections))
-    coef_own = jnp.where(low, upper_mine, lower_mine)
-    coef_other = jnp.where(low, lower_above, upper_below)
+    coef_own, _ = weights(mine, section)
+    _, coef_other = weights(under, section - 1)
     field = jnp.where(lane < 8, mine, 0.0)
-    field_other = jnp.where(lane < 8, jnp.where(low, above, below), 0.0)
-
-    for copy in image_copies:
-        copy.wait_recv()
+    field_other = jnp.where(lane < 8, under, 0.0)
+
+    @pl.when(below)
+    def _():
+        image_copy.wait_recv()
+
     other_spectrum = spectrum(other_image[...], along_x, along_u)
     cross_real, cross_imag, terms = prepare(own_spectrum, other_spectrum)
 
-    def left_of(values):
-        return pltpu.roll(values, 1, 1)
-
-    def right_of(values):
-        return pltpu.roll(values, SIZE - 1, 1)
-
-    copies = []
+    def smooth(rows):
+        current = rows[0]
+        around = (
+            jnp.where(there[-1], rows[-1], 0.0)
+            + jnp.where(there[1], rows[1], 0.0)
+            + jnp.where(column == 0, 0.0, pltpu.roll(current, 1, 1))
+            + jnp.where(column == 3, 0.0, pltpu.roll(current, SIZE - 1, 1))
+        )
+        return current + STIFF * (around - 4.0 * current)
+
+    def exchange(step, peer):
+        return pltpu.make_async_remote_copy(
+            src_ref=sent.at[step],
+            dst_ref=received.at[step, SLOT[peer]],
+            send_sem=send_sem.at[step, SLOT[peer]],
+            recv_sem=recv_sem.at[step, SLOT[peer]],
+            device_id=device(peer),
+            device_id_type=COORD,
+        )
+
     for step in range(ITERS):
         last = step == ITERS - 1
         total, moment, end = sums_of_lags(
@@ -385,102 +408,51 @@
         offset = moment / total
         mirrored = -offset - SIZE * (end / total)
         mean_own = coef_own * offset
-        share = STEP * coef_other * mirrored
         sent[step, 0] = field + STEP * mean_own
-        sent[step, 1] = share
-        peers = [peer for peer in PEERS if abs(peer[0]) < 2] if last else PEERS
-
-        def exchange(peer):
-            return pltpu.make_async_remote_copy(
-                src_ref=sent.at[step],
-                dst_ref=received.at[step, SLOT[peer]],
-                send_sem=send_sem.at[step, SLOT[peer]],
-                recv_sem=recv_sem.at[step, SLOT[peer]],
-                device_id=device(peer),
-                device_id_type=COORD,
+        sent[step, 1] = STEP * coef_other * mirrored
+        peers = LAST_PEERS if last else PEERS
+        for peer in peers:
+            when_there(peer, lambda peer=peer: exchange(step, peer).start())
+        for peer in peers:
+            when_there(
+                (-peer[0], -peer[1]), lambda peer=peer: exchange(step, peer).wait_recv()
             )
 
-        for peer in peers:
-            when_there(peer, lambda peer=peer: exchange(peer).start())
-        for peer in peers:
-            opposite = (-peer[0], -peer[1])
-            when_there(opposite, lambda peer=peer: exchange(peer).wait_recv())
-
-        def base(ds, dr):
+        def part(kind, ds, dr):
             if (ds, dr) == (0, 0):
-                return sent[step, 0]
-            return received[step, SLOT[(-ds, -dr)], 0]
-
-        def shared(ds, dr):
-            if (ds, dr) == (0, 0):
-                return sent[step, 1]
-            return received[step, SLOT[(-ds, -dr)], 1]
-
-        there = {-1: row > 0, 1: row < nrows - 1}
-        own_rows = {
-            dr: base(0, dr) + jnp.where(low, shared(-1, dr), shared(1, dr)) for dr in (-1, 0, 1)
-        }
-        mine = own_rows[0]
-        around = (
-            jnp.where(there[-1], own_rows[-1], 0.0)
-            + jnp.where(there[1], own_rows[1], 0.0)
-            + jnp.where(column == 0, 0.0, left_of(mine))
-            + jnp.where(column == 3, 0.0, right_of(mine))
-        )
-        smoothed = mine + STIFF * (around - 4.0 * mine)
+                return sent[step, kind]
+            return received[step, SLOT[(-ds, -dr)], kind]
+
+        shared = {dr: jnp.where(above, part(1, 1, dr), 0.0) for dr in (-1, 0, 1)}
+        smoothed = smooth({dr: part(0, 0, dr) + shared[dr] for dr in (-1, 0, 1)})
         if last:
-            mean = mean_own + (1.0 / STEP) * jnp.where(low, shared(-1, 0), shared(1, 0))
+            mean = mean_own + (1.0 / STEP) * shared[0]
             for k in range(2):
-                relaxed_ref[k, 0] = smoothed[:, 4 * k : 4 * k + 4]
-                mean_ref[k, 0] = mean[:, 4 * k : 4 * k + 4]
+                result_ref[k, 0] = smoothed[:, 4 * k : 4 * k + 4]
+                result_ref[2 + k, 0] = mean[:, 4 * k : 4 * k + 4]
         else:
-            other_rows = {
-                dr: jnp.where(low, base(1, dr), base(-1, dr)) + shared(0, dr) for dr in (-1, 0, 1)
-            }
-            across = jnp.where(
-                column == 1, base(-1, 0) + shared(-2, 0), base(1, 0) + shared(2, 0)
-            )
-            them = other_rows[0]
-            around = (
-                jnp.where(there[-1], other_rows[-1], 0.0)
-                + jnp.where(there[1], other_rows[1], 0.0)
-                + jnp.where(
-                    column == 0, 0.0, jnp.where(column == 2, left_of(across), left_of(them))
-                )
-                + jnp.where(
-                    column == 3, 0.0, jnp.where(column == 1, right_of(across), right_of(them))
-                )
-            )
+            smoothed_other = smooth({dr: part(0, -1, dr) + part(1, 0, dr) for dr in (-1, 0, 1)})
             field = jnp.where(lane < 8, smoothed, 0.0)
-            field_other = jnp.where(lane < 8, them + STIFF * (around - 4.0 * them), 0.0)
-
-    for copy in image_copies + first_copies:
-        copy.wait_send()
+            field_other = jnp.where((lane < 8) & below, smoothed_other, 0.0)
+
+    @pl.when(above)
+    def _():
+        first_copy.wait_send()
+        image_copy.wait_send()
+
     for step in range(ITERS):
-        for peer in PEERS:
-            if step == ITERS - 1 and abs(peer[0]) == 2:
-                continue
-            when_there(
-                peer,
-                lambda peer=peer, step=step: pltpu.make_async_remote_copy(
-                    src_ref=sent.at[step],
-                    dst_ref=received.at[step, SLOT[peer]],
-                    send_sem=send_sem.at[step, SLOT[peer]],
-                    recv_sem=recv_sem.at[step, SLOT[peer]],
-                    device_id=device(peer),
-                    device_id_type=COORD,
-                ).wait_send(),
-            )
+        for peer in LAST_PEERS if step == ITERS - 1 else PEERS:
+            when_there(peer, lambda peer=peer, step=step: exchange(step, peer).wait_send())
 
 
 def per_device(section_images, displacement, fold_mask):
     tables = jnp.asarray(make_tables())
-    result = jax.ShapeDtypeStruct((2, 1, 1, 4), F32)
-    return pl.pallas_call(
+    result = jax.ShapeDtypeStruct((4, 1, 1, 4), F32)
+    both = pl.pallas_call(
         kernel,
-        out_shape=(result, result),
-        in_specs=[pl.BlockSpec(memory_space=pl.ANY)] * 4,
-        out_specs=[pl.BlockSpec(memory_space=pltpu.VMEM)] * 2,
+        out_shape=result,
+        in_specs=[pl.BlockSpec(memory_space=pltpu.HBM)] * 4,
+        out_specs=pl.BlockSpec(memory_space=pltpu.VMEM),
         scratch_shapes=[
             pltpu.VMEM((SIZE, 512), BF16),
             pltpu.VMEM((SIZE, 512), BF16),
@@ -488,21 +460,20 @@
             pltpu.VMEM((2, 1, 1, 4), F32),
             pltpu.VMEM((2, 1, 1, 4), jnp.int32),
             pltpu.VMEM((1, SIZE), F32),
-            pltpu.VMEM((2, 1, SIZE), F32),
+            pltpu.VMEM((1, SIZE), F32),
             pltpu.VMEM((ITERS, 2, 1, SIZE), F32),
             pltpu.VMEM((ITERS, len(PEERS), 2, 1, SIZE), F32),
             pltpu.SemaphoreType.DMA((4,)),
-            pltpu.SemaphoreType.DMA((2,)),
-            pltpu.SemaphoreType.DMA((2,)),
             pltpu.SemaphoreType.DMA((2,)),
             pltpu.SemaphoreType.DMA((2,)),
             pltpu.SemaphoreType.DMA((ITERS, len(PEERS))),
             pltpu.SemaphoreType.DMA((ITERS, len(PEERS))),
         ],
         compiler_params=pltpu.CompilerParams(
-            collective_id=0, has_side_effects=True, vmem_limit_bytes=32 * 1024 * 1024
+            collective_id=0, has_side_effects=True, vmem_limit_bytes=64 * 1024 * 1024
         ),
     )(section_images[0], displacement, fold_mask, tables)
+    return both[:2], both[2:]
 
 
 def solution(mesh):

time: 61.1 us -> 48.5 us (0.79)
  the two profiles are of different devices: /device:TPU:2 before, /device:TPU:64 now
where the time goes in v1:
time: 48.5 us; the launch traced here: 48.3 us
  Pallas kernels  46.4 us (96%)
  local copies, waits for them, and re-layouts  1.24 us (3%)
  between operations  0.64 us (1%)
    pallas_call x1, Pallas kernels, per_device(): pl.pallas_call(kernel, out_shape=result, in_specs=[pl.BlockSpec(memory_sp...  46.4 us
    slice x1, local copies, waits for them, and re-layouts, per_device(): return (both[:2], both[2:])  1.24 us

profile of v1, /device:TPU:64, one launch (start us, length us, event | category | flops | bytes accessed | tf_op | source)
XLA Modules:
  0.0 48.3 jit_solution(5200991605542354528)
XLA Ops:
  0.6 46.4 %shard_map.59 = f32[4,1,1,4]{3,2,1,0:T(1,128)} custom-call(bf16[128,512]{1,0:T(8,128)(2,1)} %bitcast.1, f32[2,1,1,4]{3,2,1,0:T(1,128)} %displacement.1, s32[2,1,1,4]{3,2,1,0:T(1,128)} %fold_mask.1, bf16[6,256,256]{2,1,0:T(8,128)(2,1)} %constant.2.clone.tables), custom_call_target="tpu_custom_call" | custom-call | tf_op jit(solution)/shard_map/pallas_call | solution.py:451
  47.0 1.2 %fusion = (f32[2,1,1,4]{3,2,1,0:T(1,128)}, f32[2,1,1,4]{3,2,1,0:T(1,128)}) fusion(f32[4,1,1,4]{3,2,1,0:T(1,128)} %shard_map.59), kind=kLoop, calls=%fused_computation | loop fusion | bytes 128 | tf_op jit(solution)/shard_map/slice | solution.py:476

commit v2 on v1

--- a/solution.py
+++ b/solution.py
@@ -20,9 +20,8 @@
 BF16 = jnp.bfloat16
 COORD = pl.DeviceIdType.MESH
 
-PEERS = [(1, 0), (-1, 0), (0, 1), (0, -1), (1, 1), (1, -1), (-1, 1), (-1, -1)]
-LAST_PEERS = [(-1, 0), (0, 1), (0, -1), (-1, 1), (-1, -1)]
-SLOT = {peer: k for k, peer in enumerate(PEERS)}
+UPPER, LOWER, FAR, BESIDE = 0, 3, 6, 8
+SLOTS = 11
 
 
 def split_table(table):
@@ -264,33 +263,51 @@
 
 def kernel(
     images, displacement, fold_mask, tables, result_ref,
-    own_image, other_image, table, disp, mask, first, first_in, sent, received,
-    load_sem, image_sem, first_sem, send_sem, recv_sem,
+    own_image, image, table, disp, mask, first, first_in,
+    own_spec, spec, cross, terms, fields, coef, shares, sent, received, raised, raised_in,
+    final, final_in,
+    load_sem, image_send, image_recv, first_send, first_recv,
+    send_sem, row_sem, recv_sem, raised_send, raised_recv, final_sem, go_sem,
 ):
     section, row = lax.axis_index("sec"), lax.axis_index("row")
     sections, nrows = lax.axis_size("sec"), lax.axis_size("row")
+    role = lax.rem(section, 4)
+    is0, is1, is2, is3 = role == 0, role == 1, role == 2, role == 3
+    works = role != 2
     above, below = section < sections - 1, section > 0
-    there = {-1: row > 0, 1: row < nrows - 1}
-
-    def device(peer):
-        return (section + peer[0], row + peer[1])
-
-    def when_there(peer, action):
-        conditions = []
-        if peer[0] != 0:
-            conditions.append(above if peer[0] > 0 else below)
-        if peer[1] != 0:
-            conditions.append(there[peer[1]])
-        pl.when(functools.reduce(jnp.logical_and, conditions))(action)
+    further = section < sections - 4
+    there = {-1: row > 0, 0: None, 1: row < nrows - 1}
+
+    def both(*flags):
+        return functools.reduce(jnp.logical_and, [flag for flag in flags if flag is not None])
+
+    def either(*flags):
+        return functools.reduce(jnp.logical_or, flags)
+
+    up = jnp.where(is1, 2, 1)
+    down = jnp.where(is3, 2, 1)
+    any_lower = either(both(is0, below), is1, is3)
+    any_upper = either(is0, is1, both(is3, above))
 
     barrier = pltpu.get_barrier_semaphore()
-    for peer in PEERS:
-        when_there(
-            peer,
-            lambda peer=peer: pl.semaphore_signal(
-                barrier, inc=1, device_id=device(peer), device_id_type=COORD
-            ),
-        )
+
+    def greet(condition, ds, dr):
+        @pl.when(both(condition, there[dr]))
+        def _():
+            pl.semaphore_signal(
+                barrier, inc=1, device_id=(section + ds, row + dr), device_id_type=COORD
+            )
+
+    for dr in (0, 1, -1):
+        greet(any_lower, -down, dr)
+        greet(any_upper, up, dr)
+        greet(both(is0, below), -3, dr)
+        if dr:
+            greet(works, 0, dr)
+    greet(both(is0, below), -2, 0)
+    greet(either(is1, is2), 1, 0)
+    greet(is3, -1, 0)
+
     loads = [
         pltpu.make_async_copy(displacement, disp, load_sem.at[0]),
         pltpu.make_async_copy(fold_mask, mask, load_sem.at[1]),
@@ -305,79 +322,137 @@
     for k in range(2):
         first[:, 4 * k : 4 * k + 4] = disp[k, 0]
         first[:, 8 + 4 * k : 12 + 4 * k] = mask[k, 0].astype(F32)
+    shares[...] = jnp.zeros((2, 2, 1, SIZE), F32)
 
     def count(flag):
         return flag.astype(jnp.int32)
 
-    along = count(above) + count(below)
     beside = count(there[-1]) + count(there[1])
-    pl.semaphore_wait(barrier, along + beside + along * beside)
-
-    first_copy = pltpu.make_async_remote_copy(
-        src_ref=first,
-        dst_ref=first_in,
-        send_sem=first_sem.at[0],
-        recv_sem=first_sem.at[1],
-        device_id=device((1, 0)),
-        device_id_type=COORD,
-    )
-    image_copy = pltpu.make_async_remote_copy(
-        src_ref=images,
-        dst_ref=other_image,
-        send_sem=image_sem.at[0],
-        recv_sem=image_sem.at[1],
-        device_id=device((1, 0)),
-        device_id_type=COORD,
-    )
-
-    @pl.when(above)
-    def _():
-        first_copy.start()
-        image_copy.start()
+    triple = 1 + beside
+    awaited = jnp.where(
+        is2,
+        2 + count(further),
+        beside
+        + triple * (count(is1) * (2 + count(further)) + count(is0) * (1 + count(below)))
+        + count(is3) * (triple * (1 + count(above)) + 1),
+    )
+    pl.semaphore_wait(barrier, awaited)
+
+    def image_copy(ds, slot):
+        return pltpu.make_async_remote_copy(
+            src_ref=images,
+            dst_ref=image.at[slot],
+            send_sem=image_send.at[ds + 1],
+            recv_sem=image_recv.at[slot],
+            device_id=(section + ds, row),
+            device_id_type=COORD,
+        )
+
+    def first_copy(ds, slot):
+        return pltpu.make_async_remote_copy(
+            src_ref=first,
+            dst_ref=first_in.at[slot],
+            send_sem=first_send.at[ds + 1],
+            recv_sem=first_recv.at[slot],
+            device_id=(section + ds, row),
+            device_id_type=COORD,
+        )
+
+    providing = [(both(is3, above), 1, 0), (is2, -1, 0), (either(is0, is2), 1, 1)]
+
+    def provide(action):
+        for condition, ds, slot in providing:
+            pl.when(condition)(lambda ds=ds, slot=slot: action(ds, slot))
+
+    def start_both(ds, slot):
+        first_copy(ds, slot).start()
+        image_copy(ds, slot).start()
+
+    provide(start_both)
 
     loads[2].wait()
     loads[3].wait()
     along_x, along_u, along_v = (
         (table[0], table[1]), (table[2], table[3]), (table[4], table[5])
     )
-    own_spectrum = spectrum(own_image[...], along_x, along_u)
+    last_image = both(is2, further)
+
+    def put(ref, values):
+        for k, value in enumerate(values):
+            ref[k] = value
+
+    def get(ref):
+        return ref[0], ref[1], ref[2], ref[3]
+
+    @pl.when(works)
+    def _():
+        put(own_spec, spectrum(own_image[...], along_x, along_u))
+
+    @pl.when(last_image)
+    def _():
+        pl.semaphore_wait(go_sem, 1)
+        image_copy(2, 1).start()
+
+    @pl.when(either(both(is0, below), is1))
+    def _():
+        first_copy(1, 0).wait_recv()
+
+    @pl.when(either(is1, is3))
+    def _():
+        first_copy(1, 1).wait_recv()
+
+    @pl.when(both(is0, jnp.logical_not(below)))
+    def _():
+        first_in[0] = jnp.zeros((1, SIZE), F32)
+        for k in range(2):
+            image[k] = jnp.zeros((SIZE, 512), BF16)
 
     lane = iota((1, SIZE), 1)
     column = lane % 4
-
-    @pl.when(below)
-    def _():
-        first_copy.wait_recv()
-
-    @pl.when(jnp.logical_not(below))
-    def _():
-        first_in[...] = jnp.zeros((1, SIZE), F32)
-        other_image[...] = jnp.zeros((SIZE, 512), BF16)
-
-    mine, under = first[...], first_in[...]
+    inside = lane < 8
 
     def weights(values, position):
         aligned = pltpu.roll(values, SIZE - 8, 1)
-        both = aligned * jnp.where(
+        pair = aligned * jnp.where(
             lane < 4, (position > 0).astype(F32), (position < sections - 1).astype(F32)
         )
-        both = jnp.where(lane < 8, both, 0.0)
-        lower = jnp.where(lane < 4, both, pltpu.roll(both, 4, 1))
-        upper = jnp.where(lane < 4, pltpu.roll(both, SIZE - 4, 1), both)
-        norm = 1.0 / jnp.maximum(lower + upper, 1.0)
-        return jnp.where(lane < 8, lower * norm, 0.0), jnp.where(lane < 8, upper * norm, 0.0)
-
-    coef_own, _ = weights(mine, section)
-    _, coef_other = weights(under, section - 1)
-    field = jnp.where(lane < 8, mine, 0.0)
-    field_other = jnp.where(lane < 8, under, 0.0)
-
-    @pl.when(below)
-    def _():
-        image_copy.wait_recv()
-
-    other_spectrum = spectrum(other_image[...], along_x, along_u)
-    cross_real, cross_imag, terms = prepare(own_spectrum, other_spectrum)
+        pair = jnp.where(inside, pair, 0.0)
+        lower = jnp.where(lane < 4, pair, pltpu.roll(pair, 4, 1))
+        upper = jnp.where(lane < 4, pltpu.roll(pair, SIZE - 4, 1), pair)
+        norm = STEP / jnp.maximum(lower + upper, 1.0)
+        return jnp.where(inside, lower * norm, 0.0), jnp.where(inside, upper * norm, 0.0)
+
+    mine, firsts = first[...], (first_in[0], first_in[1])
+    lower_mine, upper_mine = weights(mine, section)
+    lower_0, upper_0 = weights(firsts[0], jnp.where(is0, section - 1, section + 1))
+    _, upper_1 = weights(firsts[1], section - 1)
+    coef[0, 0] = jnp.where(is0, lower_mine, upper_mine)
+    coef[0, 1] = jnp.where(is0, upper_0, lower_0)
+    coef[1, 0] = jnp.where(is0, lower_0, lower_mine)
+    coef[1, 1] = upper_1
+    fields[0] = jnp.where(inside, mine, 0.0)
+    fields[1] = jnp.where(inside, firsts[0], 0.0)
+    fields[2] = jnp.where(inside, firsts[1], 0.0)
+
+    def correlate(slot):
+        if slot == 0:
+            own, other = fields[0], fields[1]
+        else:
+            own, other = jnp.where(is0, fields[1], fields[0]), fields[2]
+        total, moment, end = sums_of_lags(
+            own, other, cross[slot, 0], cross[slot, 1], terms[slot], along_u, along_v
+        )
+        total = jnp.where(inside, total, 1.0)
+        offset = moment / total
+        shares[slot, 0] = coef[slot, 0] * offset
+        shares[slot, 1] = coef[slot, 1] * (-offset - SIZE * (end / total))
+
+    def ready(slot, own):
+        put(spec.at[slot], spectrum(image[slot], along_x, along_u))
+        real, imag, sums = prepare(own(), get(spec.at[slot]))
+        cross[slot, 0] = real
+        cross[slot, 1] = imag
+        terms[slot] = sums
 
     def smooth(rows):
         current = rows[0]
@@ -389,60 +464,232 @@
         )
         return current + STIFF * (around - 4.0 * current)
 
-    def exchange(step, peer):
+    def packet(step, ds, dr, slot, port):
         return pltpu.make_async_remote_copy(
             src_ref=sent.at[step],
-            dst_ref=received.at[step, SLOT[peer]],
-            send_sem=send_sem.at[step, SLOT[peer]],
-            recv_sem=recv_sem.at[step, SLOT[peer]],
-            device_id=device(peer),
+            dst_ref=received.at[step, slot],
+            send_sem=send_sem.at[step, port],
+            recv_sem=recv_sem.at[step, slot],
+            device_id=(section + ds, row + dr),
             device_id_type=COORD,
         )
 
+    def outgoing(step):
+        upwards = (either(is0, both(is3, above)), is0, None)[step]
+        downwards = (
+            either(both(is0, below), is1, is3),
+            either(both(is0, below), is1, is3),
+            either(both(is0, below), is1),
+        )[step]
+        sends = []
+        for dr in (0, 1, -1):
+            sends.append((both(downwards, there[dr]), -down, dr, UPPER + 1 - dr, 1 + dr))
+            if upwards is not None:
+                sends.append((both(upwards, there[dr]), 1, dr, LOWER + 1 - dr, 4 + dr))
+            if step == 0:
+                sends.append((both(is1, further, there[dr]), 3, dr, FAR + 1 - dr, 7 + dr))
+        for dr in (1, -1):
+            sends.append((both(works, there[dr]), 0, dr, None, None))
+        return sends
+
+    def row_packet(step, dr):
+        k = (1 - dr) // 2
+        return pltpu.make_async_remote_copy(
+            src_ref=sent.at[step],
+            dst_ref=received.at[step, BESIDE + 1 + k],
+            send_sem=row_sem.at[step, k],
+            recv_sem=recv_sem.at[step, BESIDE + 1 + k],
+            device_id=(section, row + dr),
+            device_id_type=COORD,
+        )
+
+    def act_on(step, method):
+        for condition, ds, dr, slot, port in outgoing(step):
+            def act(ds=ds, dr=dr, slot=slot, port=port):
+                copy = row_packet(step, dr) if slot is None else packet(step, ds, dr, slot, port)
+                getattr(copy, method)()
+
+            pl.when(condition)(act)
+
+    def raise_packet(step, dr):
+        return pltpu.make_async_remote_copy(
+            src_ref=raised.at[step],
+            dst_ref=raised_in.at[step, 1 - dr],
+            send_sem=raised_send.at[step, 1 - dr],
+            recv_sem=raised_recv.at[step, 1 - dr],
+            device_id=(section + 2, row + dr),
+            device_id_type=COORD,
+        )
+
+    def incoming(step):
+        uppers = (any_upper, any_upper, either(is0, both(is3, above)))[step]
+        for dr in (0, 1, -1):
+            slots = [(both(uppers, there[dr]), UPPER + 1 + dr)]
+            if step == 0:
+                slots.append((both(is0, below, there[dr]), LOWER + 1 + dr))
+                slots.append((both(is0, below, there[dr]), FAR + 1 + dr))
+            for condition, slot in slots:
+                pl.when(condition)(lambda slot=slot: packet(step, 1, 0, slot, 0).wait_recv())
+        for dr in (1, -1):
+            pl.when(both(works, there[-dr]))(lambda dr=dr: row_packet(step, dr).wait_recv())
+
+    def incoming_lower(step):
+        for dr in (0, 1, -1):
+            if step < ITERS - 1:
+                pl.when(both(is1, there[dr]))(
+                    lambda dr=dr: packet(step, 1, 0, LOWER + 1 + dr, 0).wait_recv()
+                )
+            pl.when(both(is3, there[dr]))(lambda dr=dr: raise_packet(step, -dr).wait_recv())
+
+    def correlate_0(step):
+        correlate(0)
+
+        @pl.when(is1)
+        def _():
+            raised[step] = shares[0, 1]
+            for dr in (0, 1, -1):
+                action = raise_packet(step, dr).start
+                action() if dr == 0 else pl.when(there[dr])(action)
+
+    finish_lower = None
     for step in range(ITERS):
-        last = step == ITERS - 1
-        total, moment, end = sums_of_lags(
-            field, field_other, cross_real, cross_imag, terms, along_u, along_v
-        )
-        total = jnp.where(lane < 8, total, 1.0)
-        offset = moment / total
-        mirrored = -offset - SIZE * (end / total)
-        mean_own = coef_own * offset
-        sent[step, 0] = field + STEP * mean_own
-        sent[step, 1] = STEP * coef_other * mirrored
-        peers = LAST_PEERS if last else PEERS
-        for peer in peers:
-            when_there(peer, lambda peer=peer: exchange(step, peer).start())
-        for peer in peers:
-            when_there(
-                (-peer[0], -peer[1]), lambda peer=peer: exchange(step, peer).wait_recv()
+        if step == 0:
+            @pl.when(either(is1, is3))
+            def _():
+                image_copy(1, 1).wait_recv()
+                ready(1, lambda: get(own_spec))
+                correlate(1)
+
+            @pl.when(either(both(is0, below), is1))
+            def _():
+                image_copy(1, 0).wait_recv()
+
+            @pl.when(either(is0, is1))
+            def _():
+                ready(0, lambda: get(own_spec))
+                correlate_0(0)
+        else:
+            pl.when(either(is0, is1))(lambda: correlate_0(step))
+            finish_lower()
+            pl.when(works if step == 1 else either(is1, is3))(lambda: correlate(1))
+
+        field, field_0, field_1 = fields[0], fields[1], fields[2]
+        own_0, other_0, own_1, other_1 = shares[0, 0], shares[0, 1], shares[1, 0], shares[1, 1]
+        sent[step, 0] = field + own_0 + jnp.where(is0, 0.0, own_1)
+        sent[step, 1] = jnp.where(is0, other_0, jnp.where(is1, other_1, field_1 + other_1))
+        sent[step, 2] = jnp.where(is1, other_0, field_0 + other_0 + own_1)
+        act_on(step, "start")
+
+        if step == 0:
+            @pl.when(both(is3, above))
+            def _():
+                image_copy(1, 0).wait_send()
+                pl.semaphore_signal(
+                    go_sem, inc=1, device_id=(section - 1, row), device_id_type=COORD
+                )
+
+            @pl.when(is0)
+            def _():
+                @pl.when(below)
+                def _():
+                    image_copy(1, 1).wait_recv()
+
+                ready(1, lambda: get(spec.at[0]))
+
+        incoming(step)
+
+        def beside_row(kind, dr, step=step):
+            if dr == 0:
+                return sent[step, kind]
+            return received[step, BESIDE + 1 + (1 + dr) // 2, kind]
+
+        def from_channel(channel, kind, dr, step=step):
+            return received[step, channel + 1 + dr, kind]
+
+        rows = (-1, 0, 1)
+        takes_upper = either(is0, both(is3, above))
+        from_upper = {
+            dr: jnp.where(takes_upper, from_channel(UPPER, 1, dr), 0.0) for dr in rows
+        }
+        smoothed = smooth({dr: beside_row(0, dr) + from_upper[dr] for dr in rows})
+        if step == ITERS - 1:
+            mean = (own_0 + jnp.where(is0, 0.0, own_1) + from_upper[0]) * (1.0 / STEP)
+            incoming_lower(step)
+
+            @pl.when(is3)
+            def _():
+                final[0] = smooth({dr: beside_row(1, dr) + raised_in[step, 1 + dr] for dr in rows})
+                final[1] = (other_1 + raised_in[step, 1]) * (1.0 / STEP)
+        else:
+            bounded = jnp.logical_or(below, jnp.logical_not(is0))
+            fields[0] = jnp.where(inside, smoothed, 0.0)
+
+            @pl.when(is0)
+            def _():
+                if step == 0:
+                    known = {dr: from_channel(LOWER, 0, dr) + beside_row(1, dr) for dr in rows}
+                else:
+                    known = {dr: beside_row(2, dr) for dr in rows}
+                fields[1] = jnp.where(jnp.logical_and(inside, below), smooth(known), 0.0)
+
+            @pl.when(is1)
+            def _():
+                known = {dr: from_channel(UPPER, 1, dr) + beside_row(2, dr) for dr in rows}
+                fields[1] = jnp.where(inside, smooth(known), 0.0)
+
+            def finish_lower(step=step, beside_row=beside_row, from_channel=from_channel):
+                incoming_lower(step)
+                far = {
+                    dr: beside_row(1, dr)
+                    + jnp.where(is1, from_channel(LOWER, 0, dr), raised_in[step, 1 + dr])
+                    for dr in rows
+                }
+                if step == 0:
+                    far = {
+                        dr: jnp.where(
+                            is0, from_channel(LOWER, 1, dr) + from_channel(FAR, 2, dr), far[dr]
+                        )
+                        for dr in rows
+                    }
+                fields[2] = jnp.where(jnp.logical_and(inside, bounded), smooth(far), 0.0)
+
+    final_copy = pltpu.make_async_remote_copy(
+        src_ref=final,
+        dst_ref=final_in,
+        send_sem=final_sem.at[0],
+        recv_sem=final_sem.at[1],
+        device_id=(section - 1, row),
+        device_id_type=COORD,
+    )
+
+    def finish(relaxed_row, mean_row):
+        for k in range(2):
+            result_ref[k, 0] = relaxed_row[:, 4 * k : 4 * k + 4]
+            result_ref[2 + k, 0] = mean_row[:, 4 * k : 4 * k + 4]
+
+    pl.when(is3)(final_copy.start)
+    pl.when(works)(lambda: finish(smoothed, mean))
+
+    @pl.when(is2)
+    def _():
+        final_copy.wait_recv()
+        finish(final_in[0], final_in[1])
+
+    pl.when(is3)(final_copy.wait_send)
+
+    def sent_both(ds, slot):
+        first_copy(ds, slot).wait_send()
+        if (ds, slot) != (1, 0):
+            image_copy(ds, slot).wait_send()
+
+    provide(sent_both)
+    pl.when(last_image)(lambda: image_copy(2, 1).wait_send())
+    for step in range(ITERS):
+        act_on(step, "wait_send")
+        for dr in (0, 1, -1):
+            pl.when(both(is1, there[dr]))(
+                lambda step=step, dr=dr: raise_packet(step, dr).wait_send()
             )
-
-        def part(kind, ds, dr):
-            if (ds, dr) == (0, 0):
-                return sent[step, kind]
-            return received[step, SLOT[(-ds, -dr)], kind]
-
-        shared = {dr: jnp.where(above, part(1, 1, dr), 0.0) for dr in (-1, 0, 1)}
-        smoothed = smooth({dr: part(0, 0, dr) + shared[dr] for dr in (-1, 0, 1)})
-        if last:
-            mean = mean_own + (1.0 / STEP) * shared[0]
-            for k in range(2):
-                result_ref[k, 0] = smoothed[:, 4 * k : 4 * k + 4]
-                result_ref[2 + k, 0] = mean[:, 4 * k : 4 * k + 4]
-        else:
-            smoothed_other = smooth({dr: part(0, -1, dr) + part(1, 0, dr) for dr in (-1, 0, 1)})
-            field = jnp.where(lane < 8, smoothed, 0.0)
-            field_other = jnp.where((lane < 8) & below, smoothed_other, 0.0)
-
-    @pl.when(above)
-    def _():
-        first_copy.wait_send()
-        image_copy.wait_send()
-
-    for step in range(ITERS):
-        for peer in LAST_PEERS if step == ITERS - 1 else PEERS:
-            when_there(peer, lambda peer=peer, step=step: exchange(step, peer).wait_send())
 
 
 def per_device(section_images, displacement, fold_mask):
@@ -455,19 +702,37 @@
         out_specs=pl.BlockSpec(memory_space=pltpu.VMEM),
         scratch_shapes=[
             pltpu.VMEM((SIZE, 512), BF16),
-            pltpu.VMEM((SIZE, 512), BF16),
+            pltpu.VMEM((2, SIZE, 512), BF16),
             pltpu.VMEM((6, 256, 256), BF16),
             pltpu.VMEM((2, 1, 1, 4), F32),
             pltpu.VMEM((2, 1, 1, 4), jnp.int32),
             pltpu.VMEM((1, SIZE), F32),
-            pltpu.VMEM((1, SIZE), F32),
-            pltpu.VMEM((ITERS, 2, 1, SIZE), F32),
-            pltpu.VMEM((ITERS, len(PEERS), 2, 1, SIZE), F32),
+            pltpu.VMEM((2, 1, SIZE), F32),
+            pltpu.VMEM((4, SIZE, 256), F32),
+            pltpu.VMEM((2, 4, SIZE, 256), F32),
+            pltpu.VMEM((2, 2, SIZE, 256), F32),
+            pltpu.VMEM((2, 16, SIZE), F32),
+            pltpu.VMEM((3, 1, SIZE), F32),
+            pltpu.VMEM((2, 2, 1, SIZE), F32),
+            pltpu.VMEM((2, 2, 1, SIZE), F32),
+            pltpu.VMEM((ITERS, 3, 1, SIZE), F32),
+            pltpu.VMEM((ITERS, SLOTS, 3, 1, SIZE), F32),
+            pltpu.VMEM((ITERS, 1, SIZE), F32),
+            pltpu.VMEM((ITERS, 3, 1, SIZE), F32),
+            pltpu.VMEM((2, 1, SIZE), F32),
+            pltpu.VMEM((2, 1, SIZE), F32),
+            pltpu.SemaphoreType.DMA((4,)),
             pltpu.SemaphoreType.DMA((4,)),
             pltpu.SemaphoreType.DMA((2,)),
+            pltpu.SemaphoreType.DMA((4,)),
             pltpu.SemaphoreType.DMA((2,)),
-            pltpu.SemaphoreType.DMA((ITERS, len(PEERS))),
-            pltpu.SemaphoreType.DMA((ITERS, len(PEERS))),
+            pltpu.SemaphoreType.DMA((ITERS, 9)),
+            pltpu.SemaphoreType.DMA((ITERS, 2)),
+            pltpu.SemaphoreType.DMA((ITERS, SLOTS)),
+            pltpu.SemaphoreType.DMA((ITERS, 3)),
+            pltpu.SemaphoreType.DMA((ITERS, 3)),
+            pltpu.SemaphoreType.DMA((2,)),
+            pltpu.SemaphoreType.REGULAR,
         ],
         compiler_params=pltpu.CompilerParams(
             collective_id=0, has_side_effects=True, vmem_limit_bytes=64 * 1024 * 1024

time: 48.5 us -> 47.1 us (0.971)
  the two profiles are of different devices: /device:TPU:64 before, /device:TPU:82 now
where the time goes in v2:
time: 47.1 us; the launch traced here: 46.9 us
  Pallas kernels  45 us (96%)
  local copies, waits for them, and re-layouts  1.24 us (3%)
  between operations  0.64 us (1%)
    pallas_call x1, Pallas kernels, per_device(): pl.pallas_call(kernel, out_shape=result, in_specs=[pl.BlockSpec(memory_sp...  45 us
    slice x1, local copies, waits for them, and re-layouts, per_device(): return (both[:2], both[2:])  1.24 us

profile of v2, /device:TPU:82, one launch (start us, length us, event | category | flops | bytes accessed | tf_op | source)
XLA Modules:
  0.0 46.9 jit_solution(7968798705674621206)
XLA Ops:
  0.6 45.0 %shard_map.59 = f32[4,1,1,4]{3,2,1,0:T(1,128)} custom-call(bf16[128,512]{1,0:T(8,128)(2,1)} %bitcast.1, f32[2,1,1,4]{3,2,1,0:T(1,128)} %displacement.1, s32[2,1,1,4]{3,2,1,0:T(1,128)} %fold_mask.1, bf16[6,256,256]{2,1,0:T(8,128)(2,1)} %constant.2.clone.tables), custom_call_target="tpu_custom_call" | custom-call | tf_op jit(solution)/shard_map/pallas_call | solution.py:698
  45.7 1.2 %fusion = (f32[2,1,1,4]{3,2,1,0:T(1,128)}, f32[2,1,1,4]{3,2,1,0:T(1,128)}) fusion(f32[4,1,1,4]{3,2,1,0:T(1,128)} %shard_map.59), kind=kLoop, calls=%fused_computation | loop fusion | bytes 128 | tf_op jit(solution)/shard_map/slice | solution.py:741
